TPU v7x, 32 devices: a whole 2x2x4 slice. The times are simulated.
32 devices in a mesh: groups: 2 (over y), loop: 4 (over z), enc: 2 (over x), rep: 2 (over core).
Axes of the slice: x: 2, y: 2, z: 4, core: 2. Of those that a mesh axis runs over, the one named last changes fastest.
Arguments:
- embeddings: bfloat16 [4096, 768], P(('groups', 'loop', 'rep'), 'enc'), parts along dimension 0, may hold values from -24 to 24
- head_weight: bfloat16 [768, 768], P('enc'), may hold values from -0.21875 to 0.21875
- gp_weights: float32 [4096], P('groups'), parts along dimension 0, may hold values from -24 to 24
- counts: int32 [8], P('groups'), parts along dimension 0, may hold values from 64 to 512, as said below
Outputs:
- embed_grad: bfloat16 [4096, 768], P(('groups', 'loop', 'rep'), 'enc'), parts along dimension 0
- head_grad: float32 [1536, 768], P(('groups', 'enc')), parts along dimension 0
There are 2 independent parts, one for each index of `groups`. A program takes and returns all parts, laid end to end along the dimension named above; an argument that names none is the same for every part. Nothing has to cross between parts.
Inputs may be any that keep to these rules, and one draw needn't show every extreme that they name: `counts`: some block is full and some block holds exactly 64 valid molecules.
All inputs are finite; a program needn't handle non-finite values.
Results may differ from a plain program's by a relative error of at most 0.019.
Values may be sent and summed in bfloat16 or wider, within the bound.
A program may use at most 64 MiB of HBM per device.

v0:
```python
import functools

import jax
import jax.numpy as jnp
from jax import lax
from jax.experimental import pallas as pl
from jax.experimental.pallas import tpu as pltpu
from jax.sharding import PartitionSpec as P

EPSILON = 1e-06
PARTS = 6
CHUNKS = 2
VMEM_BYTES = 60 * 1024 * 1024
MESH_ID = pl.DeviceIdType.MESH


def kernel(
    sizes,
    emb_ref,
    head_ref,
    gp_hbm,
    counts_hbm,
    embed_out,
    head_out,
    gp_ref,
    counts_ref,
    e_all,
    w_all,
    f_own,
    n_own,
    accum,
    quot,
    h_own,
    h_core,
    h_recv,
    h_send,
    h_side,
    h_full,
    e_recv,
    z_send,
    x_send,
    c_send,
    w_send,
    w_recv,
    wy_send,
    wc_send,
    wc_recv,
    in_sem,
    hc_send,
    hc_recv,
    hi_send,
    hi_recv,
    ho_send,
    hf_send,
    hf_recv,
):
    nz, nx, nc, ng = sizes
    z = lax.axis_index("loop")
    x = lax.axis_index("enc")
    c = lax.axis_index("rep")
    g = lax.axis_index("groups")
    other = 1 - c
    rows, cols = e_all.shape[3:]
    piece = rows // CHUNKS
    quarter, feats = w_all.shape[3:]
    half = quarter * ng
    width = feats // PARTS
    has_left = z > 0
    has_right = z < nz - 1

    def x_peer(j):
        return lax.rem(x + 1 + j, nx)

    def remote(src, dst, send, recv, device):
        return pltpu.make_async_remote_copy(
            src_ref=src, dst_ref=dst, send_sem=send, recv_sem=recv,
            device_id=device, device_id_type=MESH_ID,
        )

    def g_peer(i):
        return lax.rem(g + 1 + i, ng)

    def e_copy(b, cc, xx, h, send, device):
        start = h * piece if isinstance(h, int) else pl.multiple_of(h * piece, piece)
        slot = e_all.at[b, cc, xx, pl.ds(start, piece)]
        return remote(slot, slot, send, e_recv.at[b, cc, xx, h], device)

    def z_copy(b, d, h):
        return e_copy(b, c, x, h, z_send.at[d, b, h], {"loop": z + (1 if d == 0 else -1)})

    def x_copy(b, j, h):
        return e_copy(b, c, x, h, x_send.at[j, b, h], {"enc": x_peer(j)})

    def c_copy(b, xx, h):
        return e_copy(b, c, xx, h, c_send.at[b, xx, h], {"rep": other})

    def e_wait(b, cc, xx, h):
        e_copy(b, cc, xx, h, c_send.at[b, xx, h], {"rep": other}).wait_recv()

    def w_copy(xx, gg, send, device):
        slot = w_all.at[xx, c, gg]
        return remote(slot, slot, send, w_recv.at[xx, gg], device)

    def wx_copy(j):
        return w_copy(x, g, w_send.at[j], {"enc": x_peer(j)})

    def wy_copy(j, i):
        return w_copy(x_peer(j), g, wy_send.at[j, i], {"groups": g_peer(i)})

    def w_wait(xx, gg):
        w_copy(xx, gg, w_send.at[0], {"rep": other}).wait_recv()

    def wc_copy(xx, cc, gg):
        slot = w_all.at[xx, cc, gg]
        return remote(slot, slot, wc_send.at[xx, gg], wc_recv.at[xx, gg], {"rep": other})

    own_emb = pltpu.make_async_copy(emb_ref, e_all.at[z, c, x], in_sem.at[0])
    own_emb.start()
    own_head = [
        pltpu.make_async_copy(gp_hbm, gp_ref, in_sem.at[1]),
        pltpu.make_async_copy(counts_hbm, counts_ref, in_sem.at[2]),
    ]
    for copy in own_head:
        copy.start()
    for cc in range(nc):
        for gg in range(ng):
            start = (cc * ng + gg) * quarter
            own_head.append(
                pltpu.make_async_copy(
                    head_ref.at[pl.ds(start, quarter)],
                    w_all.at[x, cc, gg],
                    in_sem.at[3 + cc * ng + gg],
                )
            )
            own_head[-1].start()

    barrier = pltpu.get_barrier_semaphore()

    @pl.when(has_left)
    def _():
        pl.semaphore_signal(barrier, 1, device_id={"loop": z - 1}, device_id_type=MESH_ID)

    @pl.when(has_right)
    def _():
        pl.semaphore_signal(barrier, 1, device_id={"loop": z + 1}, device_id_type=MESH_ID)

    for j in range(nx - 1):
        pl.semaphore_signal(barrier, 1, device_id={"enc": x_peer(j)}, device_id_type=MESH_ID)
    pl.semaphore_signal(barrier, 1, device_id={"rep": other}, device_id_type=MESH_ID)

    for i in range(ng - 1):
        pl.semaphore_signal(barrier, 1, device_id={"groups": g_peer(i)}, device_id_type=MESH_ID)
    accum[...] = jnp.zeros_like(accum)
    quot[...] = jnp.zeros_like(quot)

    pl.semaphore_wait(
        barrier, nx + ng - 1 + has_left.astype(jnp.int32) + has_right.astype(jnp.int32)
    )
    own_emb.wait()
    for copy in own_head:
        copy.wait()
    for j in range(nx - 1):
        wx_copy(j).start()

    def features(b, cc):
        total = jnp.dot(
            e_all[b, cc, 0], w_all[0].reshape(cols, feats),
            preferred_element_type=jnp.float32,
        )
        for xx in range(1, nx):
            total = total + jnp.dot(
                e_all[b, cc, xx], w_all[xx].reshape(cols, feats),
                preferred_element_type=jnp.float32,
            )
        total = total.astype(jnp.bfloat16)
        wide = total.astype(jnp.float32)
        return total, jnp.sum(wide * wide, axis=1, keepdims=True)

    def eye():
        return lax.broadcasted_iota(jnp.int32, (rows, rows), 0) == lax.broadcasted_iota(
            jnp.int32, (rows, rows), 1
        )

    def weight_row(b, cc):
        place = cc * rows + lax.broadcasted_iota(jnp.int32, (1, rows), 1)
        lanes = gp_ref.shape[1]
        split = rows // lanes
        first = (b * nc + cc) * split
        held = [gp_ref[pl.ds(first + i, 1), :] for i in range(split)]
        return jnp.where(place < counts_ref[b], jnp.concatenate(held, axis=1), 0.0)

    def tile(b, cc, feat, norm):
        norm_row = jnp.sum(jnp.where(eye(), norm, 0.0), axis=0, keepdims=True)
        scores = lax.dot_general(
            f_own[...], feat, (((1,), (1,)), ((), ())), preferred_element_type=jnp.float32
        )
        both = n_own[...] + norm_row
        denom = both - scores + EPSILON
        scaled = weight_row(b, cc) * (1.0 / (denom * denom))
        quot[...] += jnp.sum(scaled * scores, axis=1, keepdims=True)
        accum[...] += jnp.dot(
            (both * scaled).astype(jnp.bfloat16), feat, preferred_element_type=jnp.float32
        )

    def at_step(s, d):
        b = z - s if d == 0 else z + s
        return b, jnp.logical_and(jnp.logical_and(b >= 0, b < nz), s >= (1 if d else 0))

    def stage_z(u, d):
        s, h = u // CHUNKS, lax.rem(u, CHUNKS)
        b, valid = at_step(s, d)

        @pl.when(valid)
        def _():
            @pl.when(s > 0)
            def _():
                e_wait(b, c, x, h)

            @pl.when(has_right if d == 0 else has_left)
            def _():
                z_copy(b, d, h).start()

            if d == 0:
                @pl.when(jnp.logical_and(s == 0, has_left))
                def _():
                    z_copy(b, 1, h).start()

            for j in range(nx - 1):
                x_copy(b, j, h).start()
            c_copy(b, x, h).start()

    def stage_x(u, d):
        s, h = u // CHUNKS, lax.rem(u, CHUNKS)
        b, valid = at_step(s, d)

        @pl.when(valid)
        def _():
            for j in range(nx - 1):
                e_wait(b, c, x_peer(j), h)
                c_copy(b, x_peer(j), h).start()

    def stage_w():
        for j in range(nx - 1):
            w_wait(x_peer(j), g)
            for i in range(ng - 1):
                wy_copy(j, i).start()
            wc_copy(x_peer(j), c, g).start()

    def stage_first():
        for j in range(nx - 1):
            for i in range(ng - 1):
                w_wait(x_peer(j), g_peer(i))
                wc_copy(x_peer(j), c, g_peer(i)).start()
        for j in range(nx - 1):
            for gg in range(ng):
                wc_copy(x_peer(j), other, gg).wait_recv()
        feat, norm = features(z, c)
        f_own[...] = feat
        n_own[...] = norm

    def stage_c(s, d):
        b, valid = at_step(s, d)

        @pl.when(valid)
        def _():
            for h in range(CHUNKS):
                for xx in range(nx):
                    e_wait(b, other, xx, h)

            @pl.loop(0, nc)
            def _(cc):
                feat, norm = features(b, cc)
                tile(b, cc, feat, norm)

    steps = nz * CHUNKS
    x_lag = 3
    c_lag = 3 + CHUNKS

    @pl.loop(0, steps + c_lag - 1)
    def _(t):
        @pl.when(t < steps)
        def _():
            stage_z(t, 0)
            stage_z(t, 1)

        @pl.when(t == 2)
        def _():
            stage_w()

        @pl.when(t == c_lag)
        def _():
            stage_first()

        @pl.when(jnp.logical_and(t >= c_lag, lax.rem(t - c_lag + CHUNKS, CHUNKS) == 0))
        def _():
            stage_c((t - c_lag) // CHUNKS, 0)
            stage_c((t - c_lag) // CHUNKS, 1)

        @pl.when(jnp.logical_and(t >= x_lag, t < steps + x_lag))
        def _():
            stage_x(t - x_lag, 0)
            stage_x(t - x_lag, 1)

    own_weight = jnp.sum(jnp.where(eye(), weight_row(z, c), 0.0), axis=1, keepdims=True)
    grad = (
        own_weight * (accum[...] - f_own[...].astype(jnp.float32) * (2.0 * quot[...]))
    ).astype(jnp.bfloat16)
    f_own[...] = grad

    middle = nz // 2
    left_side = z < middle
    inward = jnp.where(left_side, z + 1, z - 1)
    outward = jnp.where(left_side, z - 1, z + 1)
    is_middle = jnp.logical_or(z == middle - 1, z == middle)
    is_outer = jnp.logical_or(z == 0, z == nz - 1)
    spot = is_middle.astype(jnp.int32)

    def hc_copy(k):
        return remote(
            h_core.at[k], h_recv.at[k], hc_send.at[k], hc_recv.at[k], {"rep": other}
        )

    def hi_copy(k):
        return remote(
            h_send.at[k], h_side.at[spot, k], hi_send.at[k], hi_recv.at[spot, k],
            {"loop": inward},
        )

    def hi_wait(place, k):
        remote(
            h_send.at[k], h_side.at[place, k], hi_send.at[k], hi_recv.at[place, k],
            {"loop": inward},
        ).wait_recv()

    def ho_copy(k):
        slot = h_full.at[c, k]
        return remote(slot, slot, ho_send.at[k], hf_recv.at[c, k], {"loop": outward})

    def hf_copy(k):
        slot = h_full.at[c, k]
        return remote(slot, slot, hf_send.at[k], hf_recv.at[c, k], {"rep": other})

    for k in range(PARTS):
        part = lax.dot_general(
            e_all[z, c, x], f_own[:, k * width : (k + 1) * width], (((0,), (0,)), ((), ())),
            preferred_element_type=jnp.float32,
        )
        h_full_part = part.reshape(nc, half, width)

        @pl.when(c == 0)
        def _():
            h_own[k] = h_full_part[0]
            h_core[k] = h_full_part[1].astype(jnp.bfloat16)

        @pl.when(c == 1)
        def _():
            h_own[k] = h_full_part[1]
            h_core[k] = h_full_part[0].astype(jnp.bfloat16)

        hc_copy(k).start()

    for k in range(PARTS):
        hc_copy(k).wait_recv()
        h_own[k] = h_own[k] + h_recv[k].astype(jnp.float32)

        @pl.when(is_outer)
        def _():
            h_send[k] = h_own[k].astype(jnp.bfloat16)
            hi_copy(k).start()

    for k in range(PARTS):
        @pl.when(jnp.logical_not(is_outer))
        def _():
            hi_wait(0, k)
            h_send[k] = (h_own[k] + h_side[0, k].astype(jnp.float32)).astype(jnp.bfloat16)
            hi_copy(k).start()

    embed_out[...] = lax.dot_general(
        f_own[...], w_all[x].reshape(cols, feats), (((1,), (1,)), ((), ())), preferred_element_type=jnp.float32
    ).astype(jnp.bfloat16)

    for k in range(PARTS):
        @pl.when(is_middle)
        def _():
            hi_wait(1, k)
            h_full[c, k] = (
                h_send[k].astype(jnp.float32) + h_side[1, k].astype(jnp.float32)
            ).astype(jnp.bfloat16)

        @pl.when(jnp.logical_not(is_middle))
        def _():
            ho_copy(k).wait_recv()

        @pl.when(jnp.logical_not(is_outer))
        def _():
            ho_copy(k).start()

        hf_copy(k).start()

    for k in range(PARTS):
        slot = h_full.at[other, k]
        remote(slot, slot, hf_send.at[k], hf_recv.at[other, k], {"rep": other}).wait_recv()
    head_out[...] = h_full[...]

    @pl.loop(0, nz)
    def _(b):
        for h in range(CHUNKS):
            @pl.when(jnp.logical_and(b <= z, has_right))
            def _():
                z_copy(b, 0, h).wait_send()

            @pl.when(jnp.logical_and(b >= z, has_left))
            def _():
                z_copy(b, 1, h).wait_send()

            for j in range(nx - 1):
                x_copy(b, j, h).wait_send()
            for xx in range(nx):
                c_copy(b, xx, h).wait_send()

    for j in range(nx - 1):
        wx_copy(j).wait_send()
        for i in range(ng - 1):
            wy_copy(j, i).wait_send()
        for gg in range(ng):
            wc_copy(x_peer(j), c, gg).wait_send()
    for k in range(PARTS):
        hc_copy(k).wait_send()
        hi_copy(k).wait_send()
        hf_copy(k).wait_send()

        @pl.when(jnp.logical_not(is_outer))
        def _():
            ho_copy(k).wait_send()


def finish(embed_ref, head_ref, embed_out, head_out):
    cores, parts, half, width = head_ref.shape
    embed_out[...] = embed_ref[...]
    for cc in range(cores):
        for k in range(parts):
            head_out[cc * half : (cc + 1) * half, k * width : (k + 1) * width] = head_ref[
                cc, k
            ].astype(jnp.float32)


def body(embeddings, head_weight, gp_weights, counts):
    nz, nx, nc, ng = (lax.axis_size(name) for name in ("loop", "enc", "rep", "groups"))
    rows, cols = embeddings.shape
    feats = head_weight.shape[1]
    half, width = cols // nc, feats // PARTS
    if half % (16 * ng):
        raise ValueError("head rows")
    gp_rows = gp_weights.reshape(-1, 128)
    vmem = pl.BlockSpec(memory_space=pltpu.VMEM)
    hbm = pl.BlockSpec(memory_space=pltpu.HBM)
    dma = pltpu.SemaphoreType.DMA
    embed_grad, head_sum = pl.pallas_call(
        functools.partial(kernel, (nz, nx, nc, ng)),
        out_shape=(
            jax.ShapeDtypeStruct((rows, cols), jnp.bfloat16),
            jax.ShapeDtypeStruct((nc, PARTS, half, width), jnp.bfloat16),
        ),
        in_specs=[hbm, hbm, hbm, hbm],
        out_specs=(vmem, vmem),
        scratch_shapes=[
            pltpu.VMEM(gp_rows.shape, jnp.float32),
            pltpu.SMEM(counts.shape, jnp.int32),
            pltpu.VMEM((nz, nc, nx, rows, cols), jnp.bfloat16),
            pltpu.VMEM((nx, nc, ng, half // ng, feats), jnp.bfloat16),
            pltpu.VMEM((rows, feats), jnp.bfloat16),
            pltpu.VMEM((rows, 1), jnp.float32),
            pltpu.VMEM((rows, feats), jnp.float32),
            pltpu.VMEM((rows, 1), jnp.float32),
            pltpu.VMEM((PARTS, half, width), jnp.float32),
            pltpu.VMEM((PARTS, half, width), jnp.bfloat16),
            pltpu.VMEM((PARTS, half, width), jnp.bfloat16),
            pltpu.VMEM((PARTS, half, width), jnp.bfloat16),
            pltpu.VMEM((2, PARTS, half, width), jnp.bfloat16),
            pltpu.VMEM((nc, PARTS, half, width), jnp.bfloat16),
            dma((nz, nc, nx, CHUNKS)),
            dma((2, nz, CHUNKS)),
            dma((nx - 1, nz, CHUNKS)),
            dma((nz, nx, CHUNKS)),
            dma((nx - 1,)),
            dma((nx, ng)),
            dma((nx - 1, max(ng - 1, 1))),
            dma((nx, ng)),
            dma((nx, ng)),
            dma((3 + nc * ng,)),
            dma((PARTS,)),
            dma((PARTS,)),
            dma((PARTS,)),
            dma((2, PARTS)),
            dma((PARTS,)),
            dma((PARTS,)),
            dma((nc, PARTS)),
        ],
        compiler_params=pltpu.CompilerParams(
            collective_id=0, has_side_effects=True, vmem_limit_bytes=VMEM_BYTES
        ),
    )(embeddings, head_weight, gp_rows, counts)
    return pl.pallas_call(
        finish,
        out_shape=(
            jax.ShapeDtypeStruct((rows, cols), jnp.bfloat16),
            jax.ShapeDtypeStruct((cols, feats), jnp.float32),
        ),
        in_specs=[vmem, vmem],
        out_specs=(vmem, vmem),
        compiler_params=pltpu.CompilerParams(vmem_limit_bytes=VMEM_BYTES),
    )(embed_grad, head_sum)


def solution(mesh):
    placed = (P(("groups", "loop", "rep"), "enc"), P("enc", None), P("groups"), P("groups"))
    return jax.shard_map(
        body,
        mesh=mesh,
        in_specs=placed,
        out_specs=(P(("groups", "loop", "rep"), "enc"), P(("groups", "enc"), None)),
        check_vma=False,
    )
```

profile of v0, /device:TPU:0, one launch (start us, length us, event | category | flops | bytes accessed | tf_op | source)
XLA Modules:
  0.0 53.7 jit_solution(5940840254951185439)
XLA Ops:
  0.6 50.7 %shard_map.59 = (bf16[256,384]{1,0:T(8,128)(2,1)}, bf16[2,6,192,128]{3,2,1,0:T(8,128)(2,1)}) custom-call(bf16[256,384]{1,0:T(8,128)(2,1)} %emb_ref.1, bf16[384,768]{1,0:T(8,128)(2,1)} %head_ref.1, f32[16,128]{1,0:T(8,128)} %bitcast.1, s32[4]{0:T(128)} %counts_hbm.1), custom_call_target="tpu_custom_call" | custom-call | tf_op jit(solution)/shard_map/pallas_call | solution.py:458
  51.4 2.3 %shard_map.60 = (bf16[256,384]{1,0:T(8,128)(2,1)}, f32[384,768]{1,0:T(8,128)}) custom-call(bf16[256,384]{1,0:T(8,128)(2,1)} %get-tuple-element.4.embed_ref, bf16[2,6,192,128]{3,2,1,0:T(8,128)(2,1)} %get-tuple-element.5.head_ref), custom_call_target="tpu_custom_call" | custom-call | tf_op jit(solution)/shard_map/pallas_call | solution.py:503
where the time goes:
time: 53.8 us; the launch traced here: 53.7 us
  Pallas kernels  53 us (99%)
  between operations  0.64 us (1%)
    pallas_call x1, Pallas kernels, body(): pl.pallas_call(functools.partial(kernel, (nz, nx, nc, ng)), out_shape=(ja...  50.7 us
    pallas_call x1, Pallas kernels, body(): pl.pallas_call(finish, out_shape=(jax.ShapeDtypeStruct((rows, cols), jnp....  2.28 us

commit v1 on v0

--- a/solution.py
+++ b/solution.py
@@ -444,7 +444,7 @@
             ].astype(jnp.float32)
 
 
-def body(embeddings, head_weight, gp_weights, counts):
+def ring_body(embeddings, head_weight, gp_weights, counts):
     nz, nx, nc, ng = (lax.axis_size(name) for name in ("loop", "enc", "rep", "groups"))
     rows, cols = embeddings.shape
     feats = head_weight.shape[1]
@@ -512,6 +512,384 @@
     )(embed_grad, head_sum)
 
 
+LINE = 4
+PIECES = 2
+COLUMNS = 3
+
+
+def line_kernel(
+    emb_ref,
+    head_ref,
+    gp_hbm,
+    counts_hbm,
+    embed_out,
+    own_out,
+    peer_out,
+    gp_ref,
+    counts_ref,
+    e_all,
+    w_all,
+    f_all,
+    n_row,
+    n_col,
+    w_row,
+    accum,
+    quot,
+    grads,
+    in_sem,
+    e_send,
+    e_recv,
+    w_send,
+    w_recv,
+    f_send,
+    f_recv,
+    n_send,
+    n_recv,
+    h_send,
+    h_recv,
+):
+    nz, nc = LINE, 2
+    z = lax.axis_index("loop")
+    x = lax.axis_index("enc")
+    c = lax.axis_index("rep")
+    g = lax.axis_index("groups")
+    rows, cols = e_all.shape[2:]
+    piece = rows // PIECES
+    quarter, feats = w_all.shape[3:]
+    block = nc * rows
+    lanes = gp_ref.shape[1]
+    inward = jnp.where(z < nz // 2, 1, -1)
+    is_end = jnp.logical_or(z == 0, z == nz - 1)
+    is_mid = jnp.logical_not(is_end)
+    near = z + inward
+    outer = z - inward
+    second = z + 2 * inward
+    third = z + 3 * inward
+    x_dev, c_dev, g_dev = {"enc": 1 - x}, {"rep": 1 - c}, {"groups": 1 - g}
+
+    def remote(src, dst, send, recv, device):
+        return pltpu.make_async_remote_copy(
+            src_ref=src, dst_ref=dst, send_sem=send, recv_sem=recv,
+            device_id=device, device_id_type=MESH_ID,
+        )
+
+    def e_copy(side, b, h, kind, device):
+        slot = e_all.at[side, b, pl.ds(h * piece, piece)]
+        return remote(slot, slot, e_send.at[kind, h], e_recv.at[side, b, h], device)
+
+    def e_wait(side, b, h):
+        e_copy(side, b, h, 0, x_dev).wait_recv()
+
+    def w_copy(cc, gg, kind, device):
+        slot = w_all.at[1 - x, cc, gg]
+        return remote(slot, slot, w_send.at[kind], w_recv.at[cc, gg], device)
+
+    def w_first():
+        slot = w_all.at[x, c, g]
+        return remote(slot, slot, w_send.at[0], w_recv.at[c, g], x_dev)
+
+    def f_copy(b, cc):
+        slot = f_all.at[b, cc]
+        return remote(slot, slot, f_send.at[b], f_recv.at[b], c_dev)
+
+    def n_copy(b, cc):
+        slot = n_row.at[b, cc]
+        return remote(slot, slot, n_send.at[b], n_recv.at[b], c_dev)
+
+    own_emb = pltpu.make_async_copy(emb_ref, e_all.at[x, z], in_sem.at[0])
+    own_emb.start()
+    loads = []
+    for cc in range(nc):
+        for gg in range(2):
+            loads.append(
+                pltpu.make_async_copy(
+                    head_ref.at[pl.ds((cc * 2 + gg) * quarter, quarter)],
+                    w_all.at[x, cc, gg],
+                    in_sem.at[3 + cc * 2 + gg],
+                )
+            )
+    loads.append(pltpu.make_async_copy(gp_hbm, gp_ref, in_sem.at[1]))
+    loads.append(pltpu.make_async_copy(counts_hbm, counts_ref, in_sem.at[2]))
+    for copy in loads:
+        copy.start()
+
+    barrier = pltpu.get_barrier_semaphore()
+
+    def greet(device):
+        pl.semaphore_signal(barrier, 1, device_id=device, device_id_type=MESH_ID)
+
+    greet(x_dev)
+    greet(c_dev)
+    greet(g_dev)
+    greet({"loop": near})
+    greet({"loop": second})
+
+    @pl.when(is_mid)
+    def _():
+        greet({"loop": outer})
+
+    own_emb.wait()
+    for copy in loads:
+        copy.wait()
+    pl.semaphore_wait(barrier, 5 + is_mid.astype(jnp.int32))
+
+    w_first().start()
+    for h in range(PIECES):
+        e_copy(x, z, h, 0, x_dev).start()
+        e_copy(x, z, h, 1, {"loop": second}).start()
+        e_copy(x, z, h, 2, {"loop": near}).start()
+
+        @pl.when(is_mid)
+        def _():
+            e_copy(x, z, h, 3, {"loop": outer}).start()
+
+    accum[...] = jnp.zeros_like(accum)
+    quot[...] = jnp.zeros_like(quot)
+    inside = lax.broadcasted_iota(jnp.int32, (1, lanes), 1)
+    for b in range(nz):
+        for k in range(block // lanes):
+            held = gp_ref[pl.ds(b * (block // lanes) + k, 1), :]
+            w_row[b, :, k * lanes : (k + 1) * lanes] = jnp.where(
+                inside + k * lanes < counts_ref[b], held, 0.0
+            )
+
+    w_copy(c, g, 0, x_dev).wait_recv()
+    w_copy(c, g, 1, g_dev).start()
+    w_copy(c, g, 2, c_dev).start()
+    for h in range(PIECES):
+        @pl.when(is_mid)
+        def _():
+            e_wait(x, second, h)
+            e_copy(x, second, h, 4, {"loop": outer}).start()
+            e_copy(x, second, h, 5, x_dev).start()
+
+        e_wait(1 - x, z, h)
+        e_copy(1 - x, z, h, 6, {"loop": near}).start()
+
+        @pl.when(is_mid)
+        def _():
+            e_copy(1 - x, z, h, 7, {"loop": outer}).start()
+
+        @pl.when(is_end)
+        def _():
+            e_wait(x, second, h)
+            e_copy(x, second, h, 5, x_dev).start()
+
+    w_copy(c, 1 - g, 1, g_dev).wait_recv()
+    w_copy(c, 1 - g, 3, c_dev).start()
+    w_copy(1 - c, g, 2, c_dev).wait_recv()
+    w_copy(1 - c, 1 - g, 3, c_dev).wait_recv()
+
+    def features(b):
+        total = jnp.dot(
+            e_all[0, b], w_all[0].reshape(cols, feats), preferred_element_type=jnp.float32
+        ) + jnp.dot(
+            e_all[1, b], w_all[1].reshape(cols, feats), preferred_element_type=jnp.float32
+        )
+        held = total.astype(jnp.bfloat16)
+        f_all[b, c] = held
+        f_copy(b, c).start()
+        wide = held.astype(jnp.float32)
+        norm = jnp.sum(wide * wide, axis=1, keepdims=True)
+        n_col[b] = jnp.broadcast_to(norm, (rows, lanes))
+        eye = lax.broadcasted_iota(jnp.int32, (rows, rows), 0) == lax.broadcasted_iota(
+            jnp.int32, (rows, rows), 1
+        )
+        n_row[b, c] = jnp.sum(jnp.where(eye, norm, 0.0), axis=0, keepdims=True)
+        n_copy(b, c).start()
+
+    def scores_of(i, j):
+        return lax.dot_general(
+            f_all[i, c], f_all[j].reshape(block, feats), (((1,), (1,)), ((), ())),
+            preferred_element_type=jnp.float32,
+        )
+
+    def pairs(i, j, scores):
+        spread = block // lanes
+        left = jnp.concatenate([n_col[i]] * spread, axis=1)
+        right = jnp.concatenate([n_row[j, cc] for cc in range(nc)], axis=1)
+        both = left + right
+        denom = (both - scores) + EPSILON
+        scaled = w_row[j] * (1.0 / (denom * denom))
+        part = scaled * scores
+        total = part[:, :lanes]
+        for k in range(1, spread):
+            total = total + part[:, k * lanes : (k + 1) * lanes]
+        quot[i, j // 2] += total
+        return (both * scaled).astype(jnp.bfloat16)
+
+    def tiles(todo):
+        scores = scores_of(*todo[0])
+        for k, (i, j) in enumerate(todo):
+            following = scores_of(*todo[k + 1]) if k + 1 < len(todo) else None
+            weight = pairs(i, j, scores)
+            accum[i, j // 2] += jnp.dot(
+                weight, f_all[j].reshape(block, feats), preferred_element_type=jnp.float32
+            )
+            scores = following
+
+    order = [
+        z,
+        jnp.where(is_end, second, outer),
+        near,
+        jnp.where(is_end, third, second),
+    ]
+    for s in range(nz):
+        b = order[s]
+        if s > 0:
+            for h in range(PIECES):
+                for side in range(2):
+                    seen_end = jnp.logical_and(side == x, jnp.logical_or(b == second, b == third))
+                    seen_mid = jnp.logical_and(side == x, b == second)
+                    seen = jnp.where(is_end, seen_end, seen_mid)
+
+                    @pl.when(jnp.logical_not(seen))
+                    def _():
+                        e_wait(side, b, h)
+
+        features(b)
+        if s > 0:
+            tiles([(b, order[j]) for j in range(s)])
+        f_copy(b, 1 - c).wait_recv()
+        n_copy(b, 1 - c).wait_recv()
+        tiles([(order[i], b) for i in range(s + 1)])
+        if s == 0:
+            @pl.when(is_end)
+            def _():
+                for h in range(PIECES):
+                    e_wait(x, third, h)
+                    e_copy(x, third, h, 4, x_dev).start()
+
+    for b in range(nz):
+        quotient = 2.0 * jnp.sum(quot[b, 0] + quot[b, 1], axis=1, keepdims=True)
+        spread = block // nc // lanes
+        row = jnp.concatenate(
+            [
+                jnp.where(c == 0, w_row[b, :, k * lanes : (k + 1) * lanes],
+                          w_row[b, :, rows + k * lanes : rows + (k + 1) * lanes])
+                for k in range(spread)
+            ],
+            axis=1,
+        )
+        eye = lax.broadcasted_iota(jnp.int32, (rows, rows), 0) == lax.broadcasted_iota(
+            jnp.int32, (rows, rows), 1
+        )
+        own_weight = jnp.sum(jnp.where(eye, row, 0.0), axis=1, keepdims=True)
+        carried = accum[b, 0] + accum[b, 1]
+        grads[b] = (
+            own_weight * (carried - f_all[b, c].astype(jnp.float32) * quotient)
+        ).astype(jnp.bfloat16)
+
+    width = feats // COLUMNS
+
+    def h_copy(k):
+        return remote(
+            own_out.at[k], peer_out.at[k], h_send.at[k], h_recv.at[k], c_dev
+        )
+
+    for k in range(COLUMNS):
+        own_out[k] = lax.dot_general(
+            e_all[x].reshape(nz * rows, cols),
+            grads[:, :, k * width : (k + 1) * width].reshape(nz * rows, width),
+            (((0,), (0,)), ((), ())),
+            preferred_element_type=jnp.float32,
+        ).astype(jnp.bfloat16)
+        h_copy(k).start()
+
+    embed_out[...] = lax.dot_general(
+        grads[z], w_all[x].reshape(cols, feats), (((1,), (1,)), ((), ())),
+        preferred_element_type=jnp.float32,
+    ).astype(jnp.bfloat16)
+
+    w_first().wait_send()
+    for kind, device in ((1, g_dev), (2, c_dev), (3, c_dev)):
+        w_copy(c, g, kind, device).wait_send()
+    for b in range(nz):
+        f_copy(b, c).wait_send()
+        n_copy(b, c).wait_send()
+    for h in range(PIECES):
+        for kind in (0, 1, 2, 4, 5, 6):
+            e_copy(x, z, h, kind, x_dev).wait_send()
+
+        @pl.when(is_mid)
+        def _():
+            for kind in (3, 7):
+                e_copy(x, z, h, kind, x_dev).wait_send()
+
+    for k in range(COLUMNS):
+        h_copy(k).wait()
+
+
+def line_finish(embed_ref, own_ref, peer_ref, embed_out, head_out):
+    parts, _, width = own_ref.shape
+    embed_out[...] = embed_ref[...]
+    for k in range(parts):
+        head_out[:, k * width : (k + 1) * width] = own_ref[k].astype(
+            jnp.float32
+        ) + peer_ref[k].astype(jnp.float32)
+
+
+def line_body(embeddings, head_weight, gp_weights, counts):
+    nz, nc, nx, ng = LINE, 2, 2, 2
+    rows, cols = embeddings.shape
+    feats = head_weight.shape[1]
+    quarter, width = cols // (nc * ng), feats // COLUMNS
+    lanes = 128
+    gp_rows = gp_weights.reshape(-1, lanes)
+    vmem = pl.BlockSpec(memory_space=pltpu.VMEM)
+    hbm = pl.BlockSpec(memory_space=pltpu.HBM)
+    dma = pltpu.SemaphoreType.DMA
+    part = jax.ShapeDtypeStruct((COLUMNS, cols, width), jnp.bfloat16)
+    embed_grad, own, peer = pl.pallas_call(
+        line_kernel,
+        out_shape=(jax.ShapeDtypeStruct((rows, cols), jnp.bfloat16), part, part),
+        in_specs=[hbm, hbm, hbm, hbm],
+        out_specs=(vmem, vmem, vmem),
+        scratch_shapes=[
+            pltpu.VMEM(gp_rows.shape, jnp.float32),
+            pltpu.SMEM(counts.shape, jnp.int32),
+            pltpu.VMEM((nx, nz, rows, cols), jnp.bfloat16),
+            pltpu.VMEM((nx, nc, ng, quarter, feats), jnp.bfloat16),
+            pltpu.VMEM((nz, nc, rows, feats), jnp.bfloat16),
+            pltpu.VMEM((nz, nc, 1, rows), jnp.float32),
+            pltpu.VMEM((nz, rows, lanes), jnp.float32),
+            pltpu.VMEM((nz, 1, nc * rows), jnp.float32),
+            pltpu.VMEM((nz, nz // 2, rows, feats), jnp.float32),
+            pltpu.VMEM((nz, nz // 2, rows, lanes), jnp.float32),
+            pltpu.VMEM((nz, rows, feats), jnp.bfloat16),
+            dma((3 + nc * ng,)),
+            dma((8, PIECES)),
+            dma((nx, nz, PIECES)),
+            dma((4,)),
+            dma((nc, ng)),
+            dma((nz,)),
+            dma((nz,)),
+            dma((nz,)),
+            dma((nz,)),
+            dma((COLUMNS,)),
+            dma((COLUMNS,)),
+        ],
+        compiler_params=pltpu.CompilerParams(
+            collective_id=0, has_side_effects=True, vmem_limit_bytes=VMEM_BYTES
+        ),
+    )(embeddings, head_weight, gp_rows, counts)
+    return pl.pallas_call(
+        line_finish,
+        out_shape=(
+            jax.ShapeDtypeStruct((rows, cols), jnp.bfloat16),
+            jax.ShapeDtypeStruct((cols, feats), jnp.float32),
+        ),
+        in_specs=[vmem, vmem, vmem],
+        out_specs=(vmem, vmem),
+        compiler_params=pltpu.CompilerParams(vmem_limit_bytes=VMEM_BYTES),
+    )(embed_grad, own, peer)
+
+
+def body(*args):
+    sizes = tuple(lax.axis_size(name) for name in ("loop", "enc", "rep", "groups"))
+    return line_body(*args) if sizes == (LINE, 2, 2, 2) else ring_body(*args)
+
+
 def solution(mesh):
     placed = (P(("groups", "loop", "rep"), "enc"), P("enc", None), P("groups"), P("groups"))
     return jax.shard_map(

time: 53.8 us -> 42.6 us (0.79)
  Pallas kernels: 53 us -> 41.8 us
    pallas_call x2, Pallas kernels: 53 us -> 41.8 us  [the longest x1 39.3 us: line_body(): pl.pallas_call(line_kernel, out_shape=(jax.ShapeDtypeStruct((rows, cols),...]
where the time goes in v1:
time: 42.6 us; the launch traced here: 42.4 us
  Pallas kernels  41.8 us (98%)
  between operations  0.64 us (2%)
    pallas_call x1, Pallas kernels, line_body(): pl.pallas_call(line_kernel, out_shape=(jax.ShapeDtypeStruct((rows, cols),...  39.3 us
    pallas_call x1, Pallas kernels, line_body(): pl.pallas_call(line_finish, out_shape=(jax.ShapeDtypeStruct((rows, cols),...  2.45 us

profile of v1, /device:TPU:0, one launch (start us, length us, event | category | flops | bytes accessed | tf_op | source)
XLA Modules:
  0.0 42.4 jit_solution(1787259344458019156)
XLA Ops:
  0.6 39.3 %shard_map.59 = (bf16[256,384]{1,0:T(8,128)(2,1)}, bf16[3,384,256]{2,1,0:T(8,128)(2,1)}, bf16[3,384,256]{2,1,0:T(8,128)(2,1)}) custom-call(bf16[256,384]{1,0:T(8,128)(2,1)} %emb_ref.1, bf16[384,768]{1,0:T(8,128)(2,1)} %head_ref.1, f32[16,128]{1,0:T(8,128)} %bitcast.1, s32[4]{0:T(128)} %counts_hbm.1), custom_call_target="tpu_custom_call" | custom-call | tf_op jit(solution)/shard_map/pallas_call | solution.py:843
  40.0 2.5 %shard_map.60 = (bf16[256,384]{1,0:T(8,128)(2,1)}, f32[384,768]{1,0:T(8,128)}) custom-call(bf16[256,384]{1,0:T(8,128)(2,1)} %get-tuple-element.5.embed_ref, bf16[3,384,256]{2,1,0:T(8,128)(2,1)} %get-tuple-element.6.own_ref, bf16[3,384,256]{2,1,0:T(8,128)(2,1)} %get-tuple-element.7.peer_ref), custom_call_target="tpu_custom_call" | custom-call | tf_op jit(solution)/shard_map/pallas_call | solution.py:876

commit v2 on v1

--- a/solution.py
+++ b/solution.py
@@ -513,7 +513,7 @@
 
 
 LINE = 4
-PIECES = 2
+PIECES = 4
 COLUMNS = 3
 
 
@@ -622,81 +622,110 @@
     greet(c_dev)
     greet(g_dev)
     greet({"loop": near})
-    greet({"loop": second})
 
     @pl.when(is_mid)
     def _():
         greet({"loop": outer})
 
-    own_emb.wait()
     for copy in loads:
         copy.wait()
-    pl.semaphore_wait(barrier, 5 + is_mid.astype(jnp.int32))
+    own_emb.wait()
+    pl.semaphore_wait(barrier, 4 + is_mid.astype(jnp.int32))
 
     w_first().start()
     for h in range(PIECES):
-        e_copy(x, z, h, 0, x_dev).start()
-        e_copy(x, z, h, 1, {"loop": second}).start()
-        e_copy(x, z, h, 2, {"loop": near}).start()
+        e_copy(x, z, h, 0, {"loop": near}).start()
 
         @pl.when(is_mid)
         def _():
-            e_copy(x, z, h, 3, {"loop": outer}).start()
+            e_copy(x, z, h, 1, {"loop": outer}).start()
+
+        e_copy(x, z, h, 2, x_dev).start()
+
+    fourth = jnp.where(is_end, second, outer)
+    last = jnp.where(is_end, third, second)
+    half = rows // 2
+    parts = [
+        [(z, 0), (z, 1)],
+        [(fourth, 0), (fourth, 1)],
+        [(near, 0), (last, 0)],
+        [(near, 1), (last, 1)],
+    ]
 
     accum[...] = jnp.zeros_like(accum)
     quot[...] = jnp.zeros_like(quot)
     inside = lax.broadcasted_iota(jnp.int32, (1, lanes), 1)
-    for b in range(nz):
-        for k in range(block // lanes):
-            held = gp_ref[pl.ds(b * (block // lanes) + k, 1), :]
-            w_row[b, :, k * lanes : (k + 1) * lanes] = jnp.where(
-                inside + k * lanes < counts_ref[b], held, 0.0
-            )
-
-    w_copy(c, g, 0, x_dev).wait_recv()
-    w_copy(c, g, 1, g_dev).start()
-    w_copy(c, g, 2, c_dev).start()
-    for h in range(PIECES):
-        @pl.when(is_mid)
-        def _():
+    for v in range(nz):
+        for cc in range(nc):
+            for k, (b, h) in enumerate(parts[v]):
+                place = cc * rows + h * half
+                held = gp_ref[pl.ds(b * (block // lanes) + place // lanes, 1), :]
+                w_row[v, cc, :, k * half : (k + 1) * half] = jnp.where(
+                    inside + place < counts_ref[b], held, 0.0
+                )
+
+    def head_pass():
+        w_copy(c, g, 0, x_dev).wait_recv()
+        w_copy(c, g, 1, g_dev).start()
+        w_copy(c, g, 2, c_dev).start()
+
+    @pl.when(is_mid)
+    def _():
+        for h in range(PIECES):
+            e_wait(x, outer, h)
+            e_copy(x, outer, h, 3, {"loop": near}).start()
+            e_wait(x, near, h)
+            e_copy(x, near, h, 4, {"loop": outer}).start()
+            if h == PIECES // 2 - 1:
+                head_pass()
+        for h in range(PIECES):
             e_wait(x, second, h)
-            e_copy(x, second, h, 4, {"loop": outer}).start()
-            e_copy(x, second, h, 5, x_dev).start()
-
-        e_wait(1 - x, z, h)
-        e_copy(1 - x, z, h, 6, {"loop": near}).start()
-
-        @pl.when(is_mid)
-        def _():
+            e_copy(x, second, h, 5, {"loop": outer}).start()
+            e_copy(x, second, h, 6, x_dev).start()
+        for h in range(PIECES):
+            e_wait(1 - x, z, h)
             e_copy(1 - x, z, h, 7, {"loop": outer}).start()
-
-        @pl.when(is_end)
-        def _():
+            e_copy(1 - x, z, h, 8, {"loop": near}).start()
+
+    @pl.when(is_end)
+    def _():
+        head_pass()
+        for h in range(PIECES):
+            e_wait(1 - x, z, h)
+            e_copy(1 - x, z, h, 3, {"loop": near}).start()
+        for h in range(PIECES):
             e_wait(x, second, h)
-            e_copy(x, second, h, 5, x_dev).start()
+            e_copy(x, second, h, 4, x_dev).start()
 
     w_copy(c, 1 - g, 1, g_dev).wait_recv()
     w_copy(c, 1 - g, 3, c_dev).start()
     w_copy(1 - c, g, 2, c_dev).wait_recv()
     w_copy(1 - c, 1 - g, 3, c_dev).wait_recv()
 
-    def features(b):
+    def eye():
+        return lax.broadcasted_iota(jnp.int32, (rows, rows), 0) == lax.broadcasted_iota(
+            jnp.int32, (rows, rows), 1
+        )
+
+    def taken(side, v):
+        return jnp.concatenate(
+            [e_all[side, b, h * half : (h + 1) * half] for b, h in parts[v]], axis=0
+        )
+
+    def features(v):
         total = jnp.dot(
-            e_all[0, b], w_all[0].reshape(cols, feats), preferred_element_type=jnp.float32
+            taken(0, v), w_all[0].reshape(cols, feats), preferred_element_type=jnp.float32
         ) + jnp.dot(
-            e_all[1, b], w_all[1].reshape(cols, feats), preferred_element_type=jnp.float32
+            taken(1, v), w_all[1].reshape(cols, feats), preferred_element_type=jnp.float32
         )
         held = total.astype(jnp.bfloat16)
-        f_all[b, c] = held
-        f_copy(b, c).start()
+        f_all[v, c] = held
+        f_copy(v, c).start()
         wide = held.astype(jnp.float32)
         norm = jnp.sum(wide * wide, axis=1, keepdims=True)
-        n_col[b] = jnp.broadcast_to(norm, (rows, lanes))
-        eye = lax.broadcasted_iota(jnp.int32, (rows, rows), 0) == lax.broadcasted_iota(
-            jnp.int32, (rows, rows), 1
-        )
-        n_row[b, c] = jnp.sum(jnp.where(eye, norm, 0.0), axis=0, keepdims=True)
-        n_copy(b, c).start()
+        n_col[v] = jnp.broadcast_to(norm, (rows, lanes))
+        n_row[v, c] = jnp.sum(jnp.where(eye(), norm, 0.0), axis=0, keepdims=True)
+        n_copy(v, c).start()
 
     def scores_of(i, j):
         return lax.dot_general(
@@ -704,81 +733,78 @@
             preferred_element_type=jnp.float32,
         )
 
+    def wide_row(ref, j):
+        return jnp.concatenate([ref[j, cc] for cc in range(nc)], axis=1)
+
     def pairs(i, j, scores):
         spread = block // lanes
         left = jnp.concatenate([n_col[i]] * spread, axis=1)
-        right = jnp.concatenate([n_row[j, cc] for cc in range(nc)], axis=1)
-        both = left + right
+        both = left + wide_row(n_row, j)
         denom = (both - scores) + EPSILON
-        scaled = w_row[j] * (1.0 / (denom * denom))
+        scaled = wide_row(w_row, j) * (1.0 / (denom * denom))
         part = scaled * scores
         total = part[:, :lanes]
         for k in range(1, spread):
             total = total + part[:, k * lanes : (k + 1) * lanes]
-        quot[i, j // 2] += total
+        quot[i] += total
         return (both * scaled).astype(jnp.bfloat16)
 
-    def tiles(todo):
+    def finalize(i, carried):
+        quotient = 2.0 * jnp.sum(quot[i], axis=1, keepdims=True)
+        own_weight = jnp.sum(jnp.where(eye(), w_row[i, c], 0.0), axis=1, keepdims=True)
+        grads[i] = (
+            own_weight * (carried - f_all[i, c].astype(jnp.float32) * quotient)
+        ).astype(jnp.bfloat16)
+
+    def tiles(todo, final=False):
         scores = scores_of(*todo[0])
         for k, (i, j) in enumerate(todo):
             following = scores_of(*todo[k + 1]) if k + 1 < len(todo) else None
             weight = pairs(i, j, scores)
-            accum[i, j // 2] += jnp.dot(
+            carried = accum[i] + jnp.dot(
                 weight, f_all[j].reshape(block, feats), preferred_element_type=jnp.float32
             )
+            if final:
+                finalize(i, carried)
+            else:
+                accum[i] = carried
             scores = following
 
-    order = [
-        z,
-        jnp.where(is_end, second, outer),
-        near,
-        jnp.where(is_end, third, second),
-    ]
-    for s in range(nz):
-        b = order[s]
-        if s > 0:
-            for h in range(PIECES):
-                for side in range(2):
-                    seen_end = jnp.logical_and(side == x, jnp.logical_or(b == second, b == third))
-                    seen_mid = jnp.logical_and(side == x, b == second)
-                    seen = jnp.where(is_end, seen_end, seen_mid)
-
-                    @pl.when(jnp.logical_not(seen))
-                    def _():
-                        e_wait(side, b, h)
-
-        features(b)
-        if s > 0:
-            tiles([(b, order[j]) for j in range(s)])
-        f_copy(b, 1 - c).wait_recv()
-        n_copy(b, 1 - c).wait_recv()
-        tiles([(order[i], b) for i in range(s + 1)])
-        if s == 0:
+    def third_pass(some):
+        @pl.when(is_end)
+        def _():
+            for h in some:
+                e_wait(x, third, h)
+                e_copy(x, third, h, 5, x_dev).start()
+
+    def meet(v):
+        f_copy(v, 1 - c).wait_recv()
+        n_copy(v, 1 - c).wait_recv()
+
+    features(0)
+    meet(0)
+    tiles([(0, 0)])
+    third_pass(range(PIECES // 2))
+    for h in range(PIECES):
+        e_wait(1 - x, fourth, h)
+    features(1)
+    third_pass(range(PIECES // 2, PIECES))
+    tiles([(1, 0)])
+    meet(1)
+    tiles([(0, 1), (1, 1)])
+    for v in (2, 3):
+        start = (v - 2) * (PIECES // 2)
+        for h in range(start, start + PIECES // 2):
             @pl.when(is_end)
             def _():
-                for h in range(PIECES):
-                    e_wait(x, third, h)
-                    e_copy(x, third, h, 4, x_dev).start()
-
-    for b in range(nz):
-        quotient = 2.0 * jnp.sum(quot[b, 0] + quot[b, 1], axis=1, keepdims=True)
-        spread = block // nc // lanes
-        row = jnp.concatenate(
-            [
-                jnp.where(c == 0, w_row[b, :, k * lanes : (k + 1) * lanes],
-                          w_row[b, :, rows + k * lanes : rows + (k + 1) * lanes])
-                for k in range(spread)
-            ],
-            axis=1,
-        )
-        eye = lax.broadcasted_iota(jnp.int32, (rows, rows), 0) == lax.broadcasted_iota(
-            jnp.int32, (rows, rows), 1
-        )
-        own_weight = jnp.sum(jnp.where(eye, row, 0.0), axis=1, keepdims=True)
-        carried = accum[b, 0] + accum[b, 1]
-        grads[b] = (
-            own_weight * (carried - f_all[b, c].astype(jnp.float32) * quotient)
-        ).astype(jnp.bfloat16)
+                e_wait(x, near, h)
+
+            e_wait(1 - x, near, h)
+            e_wait(1 - x, last, h)
+        features(v)
+        tiles([(v, j) for j in range(v)])
+        meet(v)
+        tiles([(i, v) for i in range(v + 1)], v == 3)
 
     width = feats // COLUMNS
 
@@ -789,7 +815,7 @@
 
     for k in range(COLUMNS):
         own_out[k] = lax.dot_general(
-            e_all[x].reshape(nz * rows, cols),
+            jnp.concatenate([taken(x, v) for v in range(nz)], axis=0),
             grads[:, :, k * width : (k + 1) * width].reshape(nz * rows, width),
             (((0,), (0,)), ((), ())),
             preferred_element_type=jnp.float32,
@@ -797,7 +823,7 @@
         h_copy(k).start()
 
     embed_out[...] = lax.dot_general(
-        grads[z], w_all[x].reshape(cols, feats), (((1,), (1,)), ((), ())),
+        grads[0], w_all[x].reshape(cols, feats), (((1,), (1,)), ((), ())),
         preferred_element_type=jnp.float32,
     ).astype(jnp.bfloat16)
 
@@ -808,12 +834,12 @@
         f_copy(b, c).wait_send()
         n_copy(b, c).wait_send()
     for h in range(PIECES):
-        for kind in (0, 1, 2, 4, 5, 6):
+        for kind in (0, 2, 3, 4, 5):
             e_copy(x, z, h, kind, x_dev).wait_send()
 
         @pl.when(is_mid)
         def _():
-            for kind in (3, 7):
+            for kind in (1, 6, 7, 8):
                 e_copy(x, z, h, kind, x_dev).wait_send()
 
     for k in range(COLUMNS):
@@ -839,10 +865,10 @@
     vmem = pl.BlockSpec(memory_space=pltpu.VMEM)
     hbm = pl.BlockSpec(memory_space=pltpu.HBM)
     dma = pltpu.SemaphoreType.DMA
-    part = jax.ShapeDtypeStruct((COLUMNS, cols, width), jnp.bfloat16)
+    part = pltpu.VMEM((COLUMNS, cols, width), jnp.bfloat16)
     embed_grad, own, peer = pl.pallas_call(
         line_kernel,
-        out_shape=(jax.ShapeDtypeStruct((rows, cols), jnp.bfloat16), part, part),
+        out_shape=(pltpu.VMEM((rows, cols), jnp.bfloat16), part, part),
         in_specs=[hbm, hbm, hbm, hbm],
         out_specs=(vmem, vmem, vmem),
         scratch_shapes=[
@@ -853,12 +879,12 @@
             pltpu.VMEM((nz, nc, rows, feats), jnp.bfloat16),
             pltpu.VMEM((nz, nc, 1, rows), jnp.float32),
             pltpu.VMEM((nz, rows, lanes), jnp.float32),
-            pltpu.VMEM((nz, 1, nc * rows), jnp.float32),
-            pltpu.VMEM((nz, nz // 2, rows, feats), jnp.float32),
-            pltpu.VMEM((nz, nz // 2, rows, lanes), jnp.float32),
+            pltpu.VMEM((nz, nc, 1, rows), jnp.float32),
+            pltpu.VMEM((nz, rows, feats), jnp.float32),
+            pltpu.VMEM((nz, rows, lanes), jnp.float32),
             pltpu.VMEM((nz, rows, feats), jnp.bfloat16),
             dma((3 + nc * ng,)),
-            dma((8, PIECES)),
+            dma((9, PIECES)),
             dma((nx, nz, PIECES)),
             dma((4,)),
             dma((nc, ng)),
@@ -873,6 +899,10 @@
             collective_id=0, has_side_effects=True, vmem_limit_bytes=VMEM_BYTES
         ),
     )(embeddings, head_weight, gp_rows, counts)
+    embed_grad, own, peer = (
+        pltpu.with_memory_space_constraint(held, pltpu.VMEM)
+        for held in (embed_grad, own, peer)
+    )
     return pl.pallas_call(
         line_finish,
         out_shape=(

time: 42.6 us -> 37.8 us (0.89)
  Pallas kernels: 41.8 us -> 37.1 us
    pallas_call x1, Pallas kernels: 39.3 us -> 35.9 us  [line_body(): pl.pallas_call(line_kernel, out_shape=(pltpu.VMEM((rows, cols), jnp.bfloa...]
    pallas_call x1, Pallas kernels: 2.45 us -> 1.15 us  [line_body(): pl.pallas_call(line_finish, out_shape=(jax.ShapeDtypeStruct((rows, cols),...]
where the time goes in v2:
time: 37.8 us; the launch traced here: 37.7 us
  Pallas kernels  37.1 us (98%)
  between operations  0.64 us (2%)
    pallas_call x1, Pallas kernels, line_body(): pl.pallas_call(line_kernel, out_shape=(pltpu.VMEM((rows, cols), jnp.bfloa...  35.9 us
    pallas_call x1, Pallas kernels, line_body(): pl.pallas_call(line_finish, out_shape=(jax.ShapeDtypeStruct((rows, cols),...  1.15 us

profile of v2, /device:TPU:0, one launch (start us, length us, event | category | flops | bytes accessed | tf_op | source)
XLA Modules:
  0.0 37.7 jit_solution(9209767524243522588)
XLA Ops:
  0.6 35.9 %shard_map.59 = (bf16[256,384]{1,0:T(8,128)(2,1)S(1)}, bf16[3,384,256]{2,1,0:T(8,128)(2,1)S(1)}, bf16[3,384,256]{2,1,0:T(8,128)(2,1)S(1)}) custom-call(bf16[256,384]{1,0:T(8,128)(2,1)} %emb_ref.1, bf16[384,768]{1,0:T(8,128)(2,1)} %head_ref.1, f32[16,128]{1,0:T(8,128)} %bitcast.1, s32[4]{0:T(128)} %counts_hbm.1), custom_call_target="tpu_custom_call" | custom-call | tf_op jit(solution)/shard_map/pallas_call | solution.py:869
  36.5 1.1 %shard_map.60 = (bf16[256,384]{1,0:T(8,128)(2,1)}, f32[384,768]{1,0:T(8,128)}) custom-call(bf16[256,384]{1,0:T(8,128)(2,1)S(1)} %get-tuple-element.5.embed_ref, bf16[3,384,256]{2,1,0:T(8,128)(2,1)S(1)} %get-tuple-element.6.own_ref, bf16[3,384,256]{2,1,0:T(8,128)(2,1)S(1)} %get-tuple-element.7.peer_ref), custom_call_target="tpu_custom_call" | custom-call | tf_op jit(solution)/shard_map/pallas_call | solution.py:906

commit v3 on v2

--- a/solution.py
+++ b/solution.py
@@ -514,6 +514,7 @@
 
 LINE = 4
 PIECES = 4
+STRIPS = 3
 COLUMNS = 3
 
 
@@ -536,6 +537,9 @@
     accum,
     quot,
     grads,
+    early_sum,
+    w_col,
+    e_turned,
     in_sem,
     e_send,
     e_recv,
@@ -580,13 +584,10 @@
     def e_wait(side, b, h):
         e_copy(side, b, h, 0, x_dev).wait_recv()
 
-    def w_copy(cc, gg, kind, device):
-        slot = w_all.at[1 - x, cc, gg]
-        return remote(slot, slot, w_send.at[kind], w_recv.at[cc, gg], device)
-
-    def w_first():
-        slot = w_all.at[x, c, g]
-        return remote(slot, slot, w_send.at[0], w_recv.at[c, g], x_dev)
+    def w_copy(cc, gg, p, kind, device, side=1 - x):
+        strip = quarter // STRIPS
+        slot = w_all.at[side, cc, gg, pl.ds(p * strip, strip)]
+        return remote(slot, slot, w_send.at[kind, p], w_recv.at[cc, gg, p], device)
 
     def f_copy(b, cc):
         slot = f_all.at[b, cc]
@@ -632,7 +633,8 @@
     own_emb.wait()
     pl.semaphore_wait(barrier, 4 + is_mid.astype(jnp.int32))
 
-    w_first().start()
+    for p in range(STRIPS):
+        w_copy(c, g, p, 0, x_dev, x).start()
     for h in range(PIECES):
         e_copy(x, z, h, 0, {"loop": near}).start()
 
@@ -664,20 +666,49 @@
                     inside + place < counts_ref[b], held, 0.0
                 )
 
-    def head_pass():
-        w_copy(c, g, 0, x_dev).wait_recv()
-        w_copy(c, g, 1, g_dev).start()
-        w_copy(c, g, 2, c_dev).start()
+    def eye():
+        return lax.broadcasted_iota(jnp.int32, (rows, rows), 0) == lax.broadcasted_iota(
+            jnp.int32, (rows, rows), 1
+        )
+
+    def taken(side, v):
+        return jnp.concatenate(
+            [e_all[side, b, h * half : (h + 1) * half] for b, h in parts[v]], axis=0
+        )
+
+    def early(v):
+        own = taken(x, v)
+        early_sum[...] = jnp.dot(
+            own, w_all[x].reshape(cols, feats), preferred_element_type=jnp.float32
+        )
+        e_turned[:, v * rows : (v + 1) * rows] = own.T
+
+    early(0)
+    for v in range(nz):
+        column = jnp.sum(jnp.where(eye(), w_row[v, c], 0.0), axis=1, keepdims=True)
+        w_col[v] = jnp.broadcast_to(column, (rows, lanes))
+
+    def x_strip(p):
+        w_copy(c, g, p, 0, x_dev).wait_recv()
+        w_copy(c, g, p, 1, g_dev).start()
+        w_copy(c, g, p, 2, c_dev).start()
+
+    def g_strip(p):
+        w_copy(c, 1 - g, p, 1, g_dev).wait_recv()
+        w_copy(c, 1 - g, p, 3, c_dev).start()
 
     @pl.when(is_mid)
     def _():
-        for h in range(PIECES):
-            e_wait(x, outer, h)
-            e_copy(x, outer, h, 3, {"loop": near}).start()
-            e_wait(x, near, h)
-            e_copy(x, near, h, 4, {"loop": outer}).start()
-            if h == PIECES // 2 - 1:
-                head_pass()
+        for h in range(max(PIECES, STRIPS)):
+            if h < STRIPS:
+                x_strip(h)
+            if h < PIECES:
+                e_wait(x, outer, h)
+                e_copy(x, outer, h, 3, {"loop": near}).start()
+                e_wait(x, near, h)
+                e_copy(x, near, h, 4, {"loop": outer}).start()
+        for p in range(STRIPS):
+            g_strip(p)
         for h in range(PIECES):
             e_wait(x, second, h)
             e_copy(x, second, h, 5, {"loop": outer}).start()
@@ -689,38 +720,33 @@
 
     @pl.when(is_end)
     def _():
-        head_pass()
-        for h in range(PIECES):
-            e_wait(1 - x, z, h)
-            e_copy(1 - x, z, h, 3, {"loop": near}).start()
-        for h in range(PIECES):
-            e_wait(x, second, h)
-            e_copy(x, second, h, 4, x_dev).start()
-
-    w_copy(c, 1 - g, 1, g_dev).wait_recv()
-    w_copy(c, 1 - g, 3, c_dev).start()
-    w_copy(1 - c, g, 2, c_dev).wait_recv()
-    w_copy(1 - c, 1 - g, 3, c_dev).wait_recv()
-
-    def eye():
-        return lax.broadcasted_iota(jnp.int32, (rows, rows), 0) == lax.broadcasted_iota(
-            jnp.int32, (rows, rows), 1
-        )
-
-    def taken(side, v):
-        return jnp.concatenate(
-            [e_all[side, b, h * half : (h + 1) * half] for b, h in parts[v]], axis=0
-        )
+        for p in range(STRIPS):
+            x_strip(p)
+        for h in range(PIECES + 1):
+            if h < PIECES:
+                e_wait(1 - x, z, h)
+                e_copy(1 - x, z, h, 3, {"loop": near}).start()
+            if h < STRIPS:
+                g_strip(h)
+            if h > 0:
+                e_wait(x, second, h - 1)
+                e_copy(x, second, h - 1, 4, x_dev).start()
+
+    for p in range(STRIPS):
+        w_copy(1 - c, g, p, 2, c_dev).wait_recv()
+        w_copy(1 - c, 1 - g, p, 3, c_dev).wait_recv()
 
     def features(v):
-        total = jnp.dot(
-            taken(0, v), w_all[0].reshape(cols, feats), preferred_element_type=jnp.float32
-        ) + jnp.dot(
-            taken(1, v), w_all[1].reshape(cols, feats), preferred_element_type=jnp.float32
+        total = early_sum[...] + jnp.dot(
+            taken(1 - x, v), w_all[1 - x].reshape(cols, feats),
+            preferred_element_type=jnp.float32,
         )
         held = total.astype(jnp.bfloat16)
         f_all[v, c] = held
         f_copy(v, c).start()
+        return held
+
+    def norms(v, held):
         wide = held.astype(jnp.float32)
         norm = jnp.sum(wide * wide, axis=1, keepdims=True)
         n_col[v] = jnp.broadcast_to(norm, (rows, lanes))
@@ -751,13 +777,15 @@
 
     def finalize(i, carried):
         quotient = 2.0 * jnp.sum(quot[i], axis=1, keepdims=True)
-        own_weight = jnp.sum(jnp.where(eye(), w_row[i, c], 0.0), axis=1, keepdims=True)
+        own_weight = jnp.concatenate([w_col[i]] * (feats // lanes), axis=1)
         grads[i] = (
             own_weight * (carried - f_all[i, c].astype(jnp.float32) * quotient)
         ).astype(jnp.bfloat16)
 
-    def tiles(todo, final=False):
+    def tiles(todo, final=False, between=None):
         scores = scores_of(*todo[0])
+        if between is not None:
+            norms(*between)
         for k, (i, j) in enumerate(todo):
             following = scores_of(*todo[k + 1]) if k + 1 < len(todo) else None
             weight = pairs(i, j, scores)
@@ -777,32 +805,45 @@
                 e_wait(x, third, h)
                 e_copy(x, third, h, 5, x_dev).start()
 
+    def quarter_of(k):
+        return range(k * PIECES // 4, (k + 1) * PIECES // 4)
+
     def meet(v):
         f_copy(v, 1 - c).wait_recv()
         n_copy(v, 1 - c).wait_recv()
 
-    features(0)
+    def near_own(some):
+        @pl.when(is_end)
+        def _():
+            for h in some:
+                e_wait(x, near, h)
+
+    norms(0, features(0))
+    third_pass(quarter_of(0))
     meet(0)
     tiles([(0, 0)])
-    third_pass(range(PIECES // 2))
+    third_pass(quarter_of(1))
+    early(1)
     for h in range(PIECES):
         e_wait(1 - x, fourth, h)
-    features(1)
-    third_pass(range(PIECES // 2, PIECES))
-    tiles([(1, 0)])
+    held = features(1)
+    third_pass(quarter_of(2))
+    tiles([(1, 0)], between=(1, held))
+    third_pass(quarter_of(3))
+    near_own(range(PIECES // 2))
+    early(2)
     meet(1)
     tiles([(0, 1), (1, 1)])
     for v in (2, 3):
         start = (v - 2) * (PIECES // 2)
         for h in range(start, start + PIECES // 2):
-            @pl.when(is_end)
-            def _():
-                e_wait(x, near, h)
-
             e_wait(1 - x, near, h)
             e_wait(1 - x, last, h)
-        features(v)
-        tiles([(v, j) for j in range(v)])
+        held = features(v)
+        tiles([(v, j) for j in range(v)], between=(v, held))
+        if v == 2:
+            near_own(range(PIECES // 2, PIECES))
+            early(3)
         meet(v)
         tiles([(i, v) for i in range(v + 1)], v == 3)
 
@@ -814,10 +855,9 @@
         )
 
     for k in range(COLUMNS):
-        own_out[k] = lax.dot_general(
-            jnp.concatenate([taken(x, v) for v in range(nz)], axis=0),
+        own_out[k] = jnp.dot(
+            e_turned[...],
             grads[:, :, k * width : (k + 1) * width].reshape(nz * rows, width),
-            (((0,), (0,)), ((), ())),
             preferred_element_type=jnp.float32,
         ).astype(jnp.bfloat16)
         h_copy(k).start()
@@ -827,9 +867,9 @@
         preferred_element_type=jnp.float32,
     ).astype(jnp.bfloat16)
 
-    w_first().wait_send()
-    for kind, device in ((1, g_dev), (2, c_dev), (3, c_dev)):
-        w_copy(c, g, kind, device).wait_send()
+    for p in range(STRIPS):
+        for kind, device in ((0, x_dev), (1, g_dev), (2, c_dev), (3, c_dev)):
+            w_copy(c, g, p, kind, device).wait_send()
     for b in range(nz):
         f_copy(b, c).wait_send()
         n_copy(b, c).wait_send()
@@ -883,11 +923,14 @@
             pltpu.VMEM((nz, rows, feats), jnp.float32),
             pltpu.VMEM((nz, rows, lanes), jnp.float32),
             pltpu.VMEM((nz, rows, feats), jnp.bfloat16),
+            pltpu.VMEM((rows, feats), jnp.float32),
+            pltpu.VMEM((nz, rows, lanes), jnp.float32),
+            pltpu.VMEM((cols, nz * rows), jnp.bfloat16),
             dma((3 + nc * ng,)),
             dma((9, PIECES)),
             dma((nx, nz, PIECES)),
-            dma((4,)),
-            dma((nc, ng)),
+            dma((4, STRIPS)),
+            dma((nc, ng, STRIPS)),
             dma((nz,)),
             dma((nz,)),
             dma((nz,)),

time: 37.8 us -> 35.7 us (0.944)
  Pallas kernels: 37.1 us -> 34.9 us
    pallas_call x1, Pallas kernels: 35.9 us -> 33.7 us  [line_body(): pl.pallas_call(line_kernel, out_shape=(pltpu.VMEM((rows, cols), jnp.bfloa...]
where the time goes in v3:
time: 35.7 us; the launch traced here: 35.5 us
  Pallas kernels  34.9 us (98%)
  between operations  0.64 us (2%)
    pallas_call x1, Pallas kernels, line_body(): pl.pallas_call(line_kernel, out_shape=(pltpu.VMEM((rows, cols), jnp.bfloa...  33.7 us
    pallas_call x1, Pallas kernels, line_body(): pl.pallas_call(line_finish, out_shape=(jax.ShapeDtypeStruct((rows, cols),...  1.15 us

profile of v3, /device:TPU:0, one launch (start us, length us, event | category | flops | bytes accessed | tf_op | source)
XLA Modules:
  0.0 35.5 jit_solution(1612578413455151172)
XLA Ops:
  0.6 33.7 %shard_map.59 = (bf16[256,384]{1,0:T(8,128)(2,1)S(1)}, bf16[3,384,256]{2,1,0:T(8,128)(2,1)S(1)}, bf16[3,384,256]{2,1,0:T(8,128)(2,1)S(1)}) custom-call(bf16[256,384]{1,0:T(8,128)(2,1)} %emb_ref.1, bf16[384,768]{1,0:T(8,128)(2,1)} %head_ref.1, f32[16,128]{1,0:T(8,128)} %bitcast.1, s32[4]{0:T(128)} %counts_hbm.1), custom_call_target="tpu_custom_call" | custom-call | tf_op jit(solution)/shard_map/pallas_call | solution.py:909
  34.4 1.1 %shard_map.60 = (bf16[256,384]{1,0:T(8,128)(2,1)}, f32[384,768]{1,0:T(8,128)}) custom-call(bf16[256,384]{1,0:T(8,128)(2,1)S(1)} %get-tuple-element.5.embed_ref, bf16[3,384,256]{2,1,0:T(8,128)(2,1)S(1)} %get-tuple-element.6.own_ref, bf16[3,384,256]{2,1,0:T(8,128)(2,1)S(1)} %get-tuple-element.7.peer_ref), custom_call_target="tpu_custom_call" | custom-call | tf_op jit(solution)/shard_map/pallas_call | solution.py:949

commit v4 on v3

--- a/solution.py
+++ b/solution.py
@@ -515,7 +515,7 @@
 LINE = 4
 PIECES = 4
 STRIPS = 3
-COLUMNS = 3
+COLUMNS = 2
 
 
 def line_kernel(
@@ -638,11 +638,11 @@
     for h in range(PIECES):
         e_copy(x, z, h, 0, {"loop": near}).start()
 
-        @pl.when(is_mid)
-        def _():
+    @pl.when(is_mid)
+    def _():
+        for h in range(4):
             e_copy(x, z, h, 1, {"loop": outer}).start()
 
-        e_copy(x, z, h, 2, x_dev).start()
 
     fourth = jnp.where(is_end, second, outer)
     last = jnp.where(is_end, third, second)
@@ -676,17 +676,26 @@
             [e_all[side, b, h * half : (h + 1) * half] for b, h in parts[v]], axis=0
         )
 
-    def early(v):
-        own = taken(x, v)
-        early_sum[...] = jnp.dot(
-            own, w_all[x].reshape(cols, feats), preferred_element_type=jnp.float32
-        )
-        e_turned[:, v * rows : (v + 1) * rows] = own.T
-
-    early(0)
+    def early(b, places):
+        made = jnp.dot(
+            e_all[x, b], w_all[x].reshape(cols, feats), preferred_element_type=jnp.float32
+        )
+        for h, (v, k) in enumerate(places):
+            own = slice(h * half, (h + 1) * half)
+            early_sum[v, k * half : (k + 1) * half] = made[own]
+            spot = v * rows + k * half
+            e_turned[:, spot : spot + half] = e_all[x, b, own].T
+
+    early(z, [(0, 0), (0, 1)])
     for v in range(nz):
         column = jnp.sum(jnp.where(eye(), w_row[v, c], 0.0), axis=1, keepdims=True)
         w_col[v] = jnp.broadcast_to(column, (rows, lanes))
+
+    for p in range(STRIPS):
+        w_copy(c, g, p, 0, x_dev, x).wait_send()
+        if p == STRIPS - 1:
+            for h in range(PIECES):
+                e_copy(x, z, h, 2, x_dev).start()
 
     def x_strip(p):
         w_copy(c, g, p, 0, x_dev).wait_recv()
@@ -707,6 +716,7 @@
                 e_copy(x, outer, h, 3, {"loop": near}).start()
                 e_wait(x, near, h)
                 e_copy(x, near, h, 4, {"loop": outer}).start()
+        early(near, [(2, 0), (3, 0)])
         for p in range(STRIPS):
             g_strip(p)
         for h in range(PIECES):
@@ -722,6 +732,9 @@
     def _():
         for p in range(STRIPS):
             x_strip(p)
+        for h in range(PIECES):
+            e_wait(x, near, h)
+        early(near, [(2, 0), (3, 0)])
         for h in range(PIECES + 1):
             if h < PIECES:
                 e_wait(1 - x, z, h)
@@ -737,7 +750,7 @@
         w_copy(1 - c, 1 - g, p, 3, c_dev).wait_recv()
 
     def features(v):
-        total = early_sum[...] + jnp.dot(
+        total = early_sum[v] + jnp.dot(
             taken(1 - x, v), w_all[1 - x].reshape(cols, feats),
             preferred_element_type=jnp.float32,
         )
@@ -792,7 +805,7 @@
             carried = accum[i] + jnp.dot(
                 weight, f_all[j].reshape(block, feats), preferred_element_type=jnp.float32
             )
-            if final:
+            if final and j == nz - 1:
                 finalize(i, carried)
             else:
                 accum[i] = carried
@@ -812,26 +825,19 @@
         f_copy(v, 1 - c).wait_recv()
         n_copy(v, 1 - c).wait_recv()
 
-    def near_own(some):
-        @pl.when(is_end)
-        def _():
-            for h in some:
-                e_wait(x, near, h)
-
     norms(0, features(0))
     third_pass(quarter_of(0))
+    early(fourth, [(1, 0), (1, 1)])
     meet(0)
     tiles([(0, 0)])
     third_pass(quarter_of(1))
-    early(1)
     for h in range(PIECES):
         e_wait(1 - x, fourth, h)
     held = features(1)
     third_pass(quarter_of(2))
     tiles([(1, 0)], between=(1, held))
     third_pass(quarter_of(3))
-    near_own(range(PIECES // 2))
-    early(2)
+    early(last, [(2, 1), (3, 1)])
     meet(1)
     tiles([(0, 1), (1, 1)])
     for v in (2, 3):
@@ -841,9 +847,6 @@
             e_wait(1 - x, last, h)
         held = features(v)
         tiles([(v, j) for j in range(v)], between=(v, held))
-        if v == 2:
-            near_own(range(PIECES // 2, PIECES))
-            early(3)
         meet(v)
         tiles([(i, v) for i in range(v + 1)], v == 3)
 
@@ -868,7 +871,7 @@
     ).astype(jnp.bfloat16)
 
     for p in range(STRIPS):
-        for kind, device in ((0, x_dev), (1, g_dev), (2, c_dev), (3, c_dev)):
+        for kind, device in ((1, g_dev), (2, c_dev), (3, c_dev)):
             w_copy(c, g, p, kind, device).wait_send()
     for b in range(nz):
         f_copy(b, c).wait_send()
@@ -923,7 +926,7 @@
             pltpu.VMEM((nz, rows, feats), jnp.float32),
             pltpu.VMEM((nz, rows, lanes), jnp.float32),
             pltpu.VMEM((nz, rows, feats), jnp.bfloat16),
-            pltpu.VMEM((rows, feats), jnp.float32),
+            pltpu.VMEM((nz, rows, feats), jnp.float32),
             pltpu.VMEM((nz, rows, lanes), jnp.float32),
             pltpu.VMEM((cols, nz * rows), jnp.bfloat16),
             dma((3 + nc * ng,)),

time: 35.7 us -> 34.7 us (0.972)
  Pallas kernels: 34.9 us -> 33.9 us
    pallas_call x1, Pallas kernels: 33.7 us -> 32.8 us  [line_body(): pl.pallas_call(line_kernel, out_shape=(pltpu.VMEM((rows, cols), jnp.bfloa...]
where the time goes in v4:
time: 34.7 us; the launch traced here: 34.6 us
  Pallas kernels  33.9 us (98%)
  between operations  0.64 us (2%)
    pallas_call x1, Pallas kernels, line_body(): pl.pallas_call(line_kernel, out_shape=(pltpu.VMEM((rows, cols), jnp.bfloa...  32.8 us
    pallas_call x1, Pallas kernels, line_body(): pl.pallas_call(line_finish, out_shape=(jax.ShapeDtypeStruct((rows, cols),...  1.15 us

profile of v4, /device:TPU:0, one launch (start us, length us, event | category | flops | bytes accessed | tf_op | source)
XLA Modules:
  0.0 34.6 jit_solution(11816298014626418776)
XLA Ops:
  0.6 32.8 %shard_map.59 = (bf16[256,384]{1,0:T(8,128)(2,1)S(1)}, bf16[2,384,384]{2,1,0:T(8,128)(2,1)S(1)}, bf16[2,384,384]{2,1,0:T(8,128)(2,1)S(1)}) custom-call(bf16[256,384]{1,0:T(8,128)(2,1)} %emb_ref.1, bf16[384,768]{1,0:T(8,128)(2,1)} %head_ref.1, f32[16,128]{1,0:T(8,128)} %bitcast.1, s32[4]{0:T(128)} %counts_hbm.1), custom_call_target="tpu_custom_call" | custom-call | tf_op jit(solution)/shard_map/pallas_call | solution.py:912
  33.4 1.1 %shard_map.60 = (bf16[256,384]{1,0:T(8,128)(2,1)}, f32[384,768]{1,0:T(8,128)}) custom-call(bf16[256,384]{1,0:T(8,128)(2,1)S(1)} %get-tuple-element.5.embed_ref, bf16[2,384,384]{2,1,0:T(8,128)(2,1)S(1)} %get-tuple-element.6.own_ref, bf16[2,384,384]{2,1,0:T(8,128)(2,1)S(1)} %get-tuple-element.7.peer_ref), custom_call_target="tpu_custom_call" | custom-call | tf_op jit(solution)/shard_map/pallas_call | solution.py:952

commit v5 on v4

--- a/solution.py
+++ b/solution.py
@@ -597,6 +597,20 @@
         slot = n_row.at[b, cc]
         return remote(slot, slot, n_send.at[b], n_recv.at[b], c_dev)
 
+    barrier = pltpu.get_barrier_semaphore()
+
+    def greet(device):
+        pl.semaphore_signal(barrier, 1, device_id=device, device_id_type=MESH_ID)
+
+    greet(x_dev)
+    greet(c_dev)
+    greet(g_dev)
+    greet({"loop": near})
+
+    @pl.when(is_mid)
+    def _():
+        greet({"loop": outer})
+
     own_emb = pltpu.make_async_copy(emb_ref, e_all.at[x, z], in_sem.at[0])
     own_emb.start()
     loads = []
@@ -614,23 +628,9 @@
     for copy in loads:
         copy.start()
 
-    barrier = pltpu.get_barrier_semaphore()
-
-    def greet(device):
-        pl.semaphore_signal(barrier, 1, device_id=device, device_id_type=MESH_ID)
-
-    greet(x_dev)
-    greet(c_dev)
-    greet(g_dev)
-    greet({"loop": near})
-
-    @pl.when(is_mid)
-    def _():
-        greet({"loop": outer})
-
-    for copy in loads:
+    own_emb.wait()
+    for copy in loads[:4]:
         copy.wait()
-    own_emb.wait()
     pl.semaphore_wait(barrier, 4 + is_mid.astype(jnp.int32))
 
     for p in range(STRIPS):
@@ -654,6 +654,8 @@
         [(near, 1), (last, 1)],
     ]
 
+    for copy in loads[4:]:
+        copy.wait()
     accum[...] = jnp.zeros_like(accum)
     quot[...] = jnp.zeros_like(quot)
     inside = lax.broadcasted_iota(jnp.int32, (1, lanes), 1)

time: 34.7 us -> 34.7 us (level)
  no operation moved by 1% of the time
where the time goes in v5:
time: 34.7 us; the launch traced here: 34.5 us
  Pallas kernels  33.9 us (98%)
  between operations  0.64 us (2%)
    pallas_call x1, Pallas kernels, line_body(): pl.pallas_call(line_kernel, out_shape=(pltpu.VMEM((rows, cols), jnp.bfloa...  32.8 us
    pallas_call x1, Pallas kernels, line_body(): pl.pallas_call(line_finish, out_shape=(jax.ShapeDtypeStruct((rows, cols),...  1.15 us

profile of v5, /device:TPU:0, one launch (start us, length us, event | category | flops | bytes accessed | tf_op | source)
XLA Modules:
  0.0 34.5 jit_solution(10636968983756033026)
XLA Ops:
  0.6 32.8 %shard_map.59 = (bf16[256,384]{1,0:T(8,128)(2,1)S(1)}, bf16[2,384,384]{2,1,0:T(8,128)(2,1)S(1)}, bf16[2,384,384]{2,1,0:T(8,128)(2,1)S(1)}) custom-call(bf16[256,384]{1,0:T(8,128)(2,1)} %emb_ref.1, bf16[384,768]{1,0:T(8,128)(2,1)} %head_ref.1, f32[16,128]{1,0:T(8,128)} %bitcast.1, s32[4]{0:T(128)} %counts_hbm.1), custom_call_target="tpu_custom_call" | custom-call | tf_op jit(solution)/shard_map/pallas_call | solution.py:914
  33.4 1.1 %shard_map.60 = (bf16[256,384]{1,0:T(8,128)(2,1)}, f32[384,768]{1,0:T(8,128)}) custom-call(bf16[256,384]{1,0:T(8,128)(2,1)S(1)} %get-tuple-element.5.embed_ref, bf16[2,384,384]{2,1,0:T(8,128)(2,1)S(1)} %get-tuple-element.6.own_ref, bf16[2,384,384]{2,1,0:T(8,128)(2,1)S(1)} %get-tuple-element.7.peer_ref), custom_call_target="tpu_custom_call" | custom-call | tf_op jit(solution)/shard_map/pallas_call | solution.py:954

commit v6 on v5

--- a/solution.py
+++ b/solution.py
@@ -831,8 +831,8 @@
     third_pass(quarter_of(0))
     early(fourth, [(1, 0), (1, 1)])
     meet(0)
+    third_pass(quarter_of(1))
     tiles([(0, 0)])
-    third_pass(quarter_of(1))
     for h in range(PIECES):
         e_wait(1 - x, fourth, h)
     held = features(1)

time: 34.7 us -> 34.7 us (level)
  no operation moved by 1% of the time
where the time goes in v6:
time: 34.7 us; the launch traced here: 34.5 us
  Pallas kernels  33.9 us (98%)
  between operations  0.64 us (2%)
    pallas_call x1, Pallas kernels, line_body(): pl.pallas_call(line_kernel, out_shape=(pltpu.VMEM((rows, cols), jnp.bfloa...  32.7 us
    pallas_call x1, Pallas kernels, line_body(): pl.pallas_call(line_finish, out_shape=(jax.ShapeDtypeStruct((rows, cols),...  1.15 us

profile of v6, /device:TPU:0, one launch (start us, length us, event | category | flops | bytes accessed | tf_op | source)
XLA Modules:
  0.0 34.5 jit_solution(1344949657316675851)
XLA Ops:
  0.6 32.7 %shard_map.59 = (bf16[256,384]{1,0:T(8,128)(2,1)S(1)}, bf16[2,384,384]{2,1,0:T(8,128)(2,1)S(1)}, bf16[2,384,384]{2,1,0:T(8,128)(2,1)S(1)}) custom-call(bf16[256,384]{1,0:T(8,128)(2,1)} %emb_ref.1, bf16[384,768]{1,0:T(8,128)(2,1)} %head_ref.1, f32[16,128]{1,0:T(8,128)} %bitcast.1, s32[4]{0:T(128)} %counts_hbm.1), custom_call_target="tpu_custom_call" | custom-call | tf_op jit(solution)/shard_map/pallas_call | solution.py:914
  33.4 1.1 %shard_map.60 = (bf16[256,384]{1,0:T(8,128)(2,1)}, f32[384,768]{1,0:T(8,128)}) custom-call(bf16[256,384]{1,0:T(8,128)(2,1)S(1)} %get-tuple-element.5.embed_ref, bf16[2,384,384]{2,1,0:T(8,128)(2,1)S(1)} %get-tuple-element.6.own_ref, bf16[2,384,384]{2,1,0:T(8,128)(2,1)S(1)} %get-tuple-element.7.peer_ref), custom_call_target="tpu_custom_call" | custom-call | tf_op jit(solution)/shard_map/pallas_call | solution.py:954
